TPU v7x, 128 devices: a whole 4x4x4 slice. The times are simulated.
128 devices in a mesh: dp: 64 (over y, z_hi, x, core), mp: 2 (over z_lo).
Axes of the slice: x: 4, y: 4, z: 4 (z_hi: 2, z_lo: 2; z = z_hi * 2 + z_lo), core: 2. Of those that a mesh axis runs over, the one named last changes fastest.
Arguments:
- img_feat: bfloat16 [13312, 1152], P('dp'), may hold values from -16 to 16
- img_head: bfloat16 [1152, 1152], P(None, 'mp'), may hold values from -0.1875 to 0.1875
- txt_feat: bfloat16 [13312, 1152], P('dp'), may hold values from -6 to 6
- txt_head: bfloat16 [1152, 1152], P('mp'), may hold values from -0.1875 to 0.1875
Outputs:
- grad_img: float32 [13312, 1152], P('dp', 'mp')
- grad_img_head: float32 [1152, 1152], P('dp', 'mp')
- grad_txt: float32 [13312, 1152], P('dp', 'mp')
- grad_txt_head: float32 [1152, 1152], P('mp', 'dp')
All inputs are finite; a program needn't handle non-finite values.
Results may differ from a plain program's by a relative error of at most 0.014.
Values may be sent and summed in bfloat16 or wider, within the bound.
A program may use at most 128 MiB of HBM per device.

v0:
```python
import jax
import jax.numpy as jnp
from jax import lax
from jax.sharding import PartitionSpec as P

LOGIT_SCALE = 10.0
LOGIT_BIAS = -2.5
NORM_EPS = 1e-06


def shifted(x, axis, by):
    devices = lax.axis_size(axis)
    return lax.ppermute(x, axis, [(i, (i + by) % devices) for i in range(devices)])


def pair_terms(local, piece, local_ids, piece_ids):
    scores = lax.dot_general(
        local, piece, (((1,), (1,)), ((), ())), preferred_element_type=jnp.float32
    )
    logits = LOGIT_SCALE * scores + LOGIT_BIAS
    match = (local_ids[:, None] == piece_ids[None, :]).astype(jnp.float32)
    weights = (jax.nn.sigmoid(logits) - match).astype(jnp.bfloat16)
    return LOGIT_SCALE * jnp.dot(weights, piece, preferred_element_type=jnp.float32)


def block_ids(source, half_index, pairs, count):
    return source * pairs + half_index * count + jnp.arange(count, dtype=jnp.int32)


def per_device(img_feat, img_head, txt_feat, txt_head):
    pairs = img_feat.shape[0]
    width = img_feat.shape[1]
    groups = lax.axis_size("mp")
    shards = lax.axis_size("dp")
    count = pairs // groups
    half = width // groups
    half_index = lax.axis_index("mp")
    shard_index = lax.axis_index("dp")
    img_half = jnp.dot(img_feat, img_head, preferred_element_type=jnp.float32).astype(jnp.bfloat16)
    img_proj = lax.all_gather(img_half, "mp", axis=1, tiled=True)
    img_wide = img_proj.astype(jnp.float32)
    img_scale = lax.rsqrt(jnp.sum(img_wide * img_wide, -1, keepdims=True) + NORM_EPS)
    img_emb = (img_wide * img_scale).astype(jnp.bfloat16)
    txt_wide = txt_feat.astype(jnp.float32)
    row_mean = jnp.mean(txt_wide, -1, keepdims=True)
    centered = txt_wide - row_mean
    txt_rscale = lax.rsqrt(jnp.mean(centered * centered, -1, keepdims=True) + NORM_EPS)
    txt_norm = centered * txt_rscale
    norm_half = lax.dynamic_slice_in_dim(txt_norm, half_index * half, half, 1)
    norm_half_b = norm_half.astype(jnp.bfloat16)
    txt_proj = lax.psum_scatter(
        jnp.dot(norm_half_b, txt_head, preferred_element_type=jnp.float32),
        "mp",
        scatter_dimension=0,
        tiled=True,
    )
    txt_scale = lax.rsqrt(jnp.sum(txt_proj * txt_proj, -1, keepdims=True) + NORM_EPS)
    txt_own = (txt_proj * txt_scale).astype(jnp.bfloat16)
    txt_emb = lax.all_gather(txt_own, "mp", axis=0, tiled=True)
    img_own = lax.dynamic_slice_in_dim(img_emb, half_index * count, count, 0)
    own_ids = shard_index * pairs + jnp.arange(pairs, dtype=jnp.int32)
    first_ids = block_ids(shard_index, half_index, pairs, count)
    img_start = pair_terms(img_emb, txt_own, own_ids, first_ids)
    txt_start = pair_terms(txt_emb, img_own, own_ids, first_ids)

    def text_step(offset, state):
        text_piece, img_carry = state
        text_piece = shifted(text_piece, "dp", 1)
        piece_ids = block_ids((shard_index - offset) % shards, half_index, pairs, count)
        return (text_piece, img_carry + pair_terms(img_emb, text_piece, own_ids, piece_ids))

    def image_step(offset, state):
        image_piece, txt_carry = state
        image_piece = shifted(image_piece, "dp", 1)
        piece_ids = block_ids((shard_index - offset) % shards, half_index, pairs, count)
        return (image_piece, txt_carry + pair_terms(txt_emb, image_piece, own_ids, piece_ids))

    img_acc = lax.fori_loop(1, shards, text_step, (txt_own, img_start))[1]
    txt_acc = lax.fori_loop(1, shards, image_step, (img_own, txt_start))[1]
    txt_grad_own = lax.psum_scatter(
        txt_acc.astype(jnp.bfloat16), "mp", scatter_dimension=0, tiled=True
    ).astype(jnp.float32)
    img_wide_half = lax.dynamic_slice_in_dim(img_wide, half_index * half, half, 1)
    grad_whole = lax.psum(img_acc.astype(jnp.bfloat16), "mp").astype(jnp.float32)
    img_dot = jnp.sum(img_wide * grad_whole, -1, keepdims=True)
    grad_half = lax.dynamic_slice_in_dim(grad_whole, half_index * half, half, 1)
    proj_grad = img_scale * grad_half - img_scale**3 * img_wide_half * img_dot
    proj_grad_b = proj_grad.astype(jnp.bfloat16)
    img_head_term = jnp.dot(img_feat.T, proj_grad_b, preferred_element_type=jnp.float32)
    img_input_term = jnp.dot(proj_grad_b, img_head.T, preferred_element_type=jnp.float32)
    grad_img = lax.psum_scatter(
        img_input_term.astype(jnp.bfloat16), "mp", scatter_dimension=1, tiled=True
    ).astype(jnp.float32)
    txt_dot = jnp.sum(txt_proj * txt_grad_own, -1, keepdims=True)
    txt_proj_grad_own = (txt_scale * txt_grad_own - txt_scale**3 * txt_proj * txt_dot).astype(
        jnp.bfloat16
    )
    txt_proj_grad = lax.all_gather(txt_proj_grad_own, "mp", axis=0, tiled=True)
    txt_head_term = jnp.dot(norm_half_b.T, txt_proj_grad, preferred_element_type=jnp.float32)
    norm_grad = jnp.dot(txt_proj_grad, txt_head.T, preferred_element_type=jnp.float32)
    first_sum, second_sum = lax.psum(
        (jnp.sum(norm_grad, -1), jnp.sum(norm_grad * norm_half, -1)), "mp"
    )
    first_mean = first_sum[:, None] / width
    second_mean = second_sum[:, None] / width
    grad_txt = txt_rscale * (norm_grad - first_mean - norm_half * second_mean)
    grad_img_head, grad_txt_head = (
        lax.psum_scatter(img_head_term, "dp", scatter_dimension=0, tiled=True),
        lax.psum_scatter(txt_head_term, "dp", scatter_dimension=1, tiled=True),
    )
    return (grad_img, grad_img_head, grad_txt, grad_txt_head)


def solution(mesh):
    in_specs = (P("dp", None), P(None, "mp"), P("dp", None), P("mp", None))
    out_specs = (P("dp", "mp"), P("dp", "mp"), P("dp", "mp"), P("mp", "dp"))
    return jax.shard_map(
        per_device, mesh=mesh, in_specs=in_specs, out_specs=out_specs, check_vma=False
    )
```

profile of v0, /device:TPU:1, one launch (start us, length us, event | category | flops | bytes accessed | tf_op | source)
XLA Modules:
  0.0 2339.0 jit_solution(1156578059971605697)
XLA Ops:
  25.0 11.8 reduce-scatter.15.cloned.1.call-done
  49.2 813.6 %while.36 = (s32[]{:T(128)}, bf16[104,1152]{1,0:T(8,128)(2,1)}, f32[208,1152]{1,0:T(8,128)S(1)}, bf16[208,1152]{1,0:T(8,128)(2,1)S(1)}, s32[]{:T(128)}, /*index=...) while((s32[]{:T(128)}, bf16[104,1152]{1,0:T(8,128)(2,1)}, ...), condition=%wide.region_6.7_spmd.clone, body=%wide.region_5.6_spmd.clone.sunk | while | flops 100354504 | bytes 4076278 | solution.py:78
  66.7 11.4 collective-permute-done
  79.8 11.4 collective-permute-done
  92.8 11.4 collective-permute-done
  105.9 11.4 collective-permute-done
  118.9 11.4 collective-permute-done
  132.0 11.4 collective-permute-done
  145.0 11.4 collective-permute-done
  158.1 11.4 collective-permute-done
  171.1 11.4 collective-permute-done
  184.2 11.4 collective-permute-done
  197.2 11.4 collective-permute-done
  210.3 11.4 collective-permute-done
  223.3 11.4 collective-permute-done
  236.4 11.4 collective-permute-done
  249.4 11.4 collective-permute-done
  262.5 11.4 collective-permute-done
  275.6 11.4 collective-permute-done
  288.6 11.4 collective-permute-done
  301.7 11.4 collective-permute-done
  314.7 11.4 collective-permute-done
  327.8 11.4 collective-permute-done
  340.8 11.4 collective-permute-done
  353.9 11.4 collective-permute-done
  366.9 11.4 collective-permute-done
  380.0 11.4 collective-permute-done
  393.0 11.4 collective-permute-done
  406.1 11.4 collective-permute-done
  419.1 11.4 collective-permute-done
  432.2 11.4 collective-permute-done
  445.2 11.4 collective-permute-done
  458.3 11.4 collective-permute-done
  484.4 11.4 collective-permute-done
  510.5 11.4 collective-permute-done
  549.7 11.4 collective-permute-done
  575.8 11.4 collective-permute-done
  601.9 11.4 collective-permute-done
  641.0 11.4 collective-permute-done
  667.1 11.4 collective-permute-done
  732.4 11.4 collective-permute-done
  758.5 11.4 collective-permute-done
  797.7 11.4 collective-permute-done
  823.8 11.4 collective-permute-done
  849.9 11.4 collective-permute-done
  864.6 767.2 %while.37 = (s32[]{:T(128)}, bf16[104,1152]{1,0:T(8,128)(2,1)S(1)}, f32[208,1152]{1,0:T(8,128)S(1)}, bf16[208,1152]{1,0:T(8,128)(2,1)S(1)}, s32[]{:T(128)}, /*in...) while((s32[]{:T(128)}, bf16[104,1152]{1,0:T(8,128)(2,1)S(1)}, ...), condition=%wide.region_12.13_spmd.clone, body=%wide.region_11.12_spmd.clone.sunk | while | flops 100354504 | bytes 4076278 | solution.py:79
  1639.2 13.6 reduce-scatter.17.cloned.1.call-done
  1676.0 653.0 %all-reduce.11.cloned.1.call-done = (f32[1152,576]{0,1:T(8,128)}, f32[576,1152]{0,1:T(8,128)}) async-done(((f32[1152,576]{0,1:T(8,128)}, f32[576,1152]{0,1:T(8,128)}), (f32[1152,576]{0,1:T(8,128)}, f32[576,1152]{0,1:T(8,128)})) %all-reduce.11.cloned.1.call-update) | async-done | bytes 5308432
  (792 shorter events, 1146.1 us)
Async XLA Ops:
  7.2 29.6 %reduce-scatter.15.cloned.1.call-start = ((), (), s32[]{:S(2)}) async-start(), calls=%async_computation.5 | async-start | bytes 1437696
  11.5 1621.3 %all-reduce.9.cloned.1.call-start = ((), (), s32[]{:S(2)}) async-start(), calls=%async_computation.3 | async-start | bytes 958464 | tf_op jit(solution)/shard_map/psum | solution.py:84
  66.6 11.6 collective-permute-start
  79.6 11.6 collective-permute-start
  92.7 11.6 collective-permute-start
  105.7 11.6 collective-permute-start
  118.8 11.6 collective-permute-start
  131.8 11.6 collective-permute-start
  144.9 11.6 collective-permute-start
  157.9 11.6 collective-permute-start
  171.0 11.6 collective-permute-start
  184.1 11.6 collective-permute-start
  197.1 11.6 collective-permute-start
  210.2 11.6 collective-permute-start
  223.2 11.6 collective-permute-start
  236.3 11.6 collective-permute-start
  249.3 11.6 collective-permute-start
  262.4 11.6 collective-permute-start
  275.4 11.6 collective-permute-start
  288.5 11.6 collective-permute-start
  301.5 11.6 collective-permute-start
  314.6 11.6 collective-permute-start
  327.6 11.6 collective-permute-start
  340.7 11.6 collective-permute-start
  353.7 11.6 collective-permute-start
  366.8 11.6 collective-permute-start
  379.8 11.6 collective-permute-start
  392.9 11.6 collective-permute-start
  405.9 11.6 collective-permute-start
  419.0 11.6 collective-permute-start
  432.1 11.6 collective-permute-start
  445.1 11.6 collective-permute-start
  458.2 11.6 collective-permute-start
  471.2 11.6 collective-permute-start
  484.3 11.6 collective-permute-start
  497.3 11.6 collective-permute-start
  510.4 11.6 collective-permute-start
  523.4 11.6 collective-permute-start
  536.5 11.6 collective-permute-start
  549.5 11.6 collective-permute-start
  562.6 11.6 collective-permute-start
  575.6 11.6 collective-permute-start
  588.7 11.6 collective-permute-start
  640.9 11.6 collective-permute-start
  797.5 11.6 collective-permute-start
  863.7 789.1 %reduce-scatter.17.cloned.1.call-start = ((), (), s32[]{:S(2)}) async-start(), calls=%async_computation.6 | async-start | bytes 718848
  1632.7 41.3 %reduce-scatter.13.cloned.1.call-start = ((), (), s32[]{:S(2)}) async-start(), calls=%async_computation.4 | async-start | bytes 884736
  1639.2 689.9 %all-reduce.11.cloned.1.call-start = ((), (), s32[]{:S(2)}) async-start(), calls=%async_computation.7 | async-start | bytes 11206656
  (95 other events, 991.8 us)
Sparse Core Ops, SparseCore 0:
  11.6 25.1 reduce-scatter.14
  863.8 37.6 all-reduce.8
  1632.8 19.8 reduce-scatter.16
  1655.1 18.8 reduce-scatter.12
  1676.5 652.5 all-reduce.10
where the time goes:
time: 2340 us
  waiting for transfers between devices  2090 us (89%)
  matrix products  111 us (5%)
  local copies, waits for them, and re-layouts  54.4 us (2%)
  blocking collectives  28.4 us (1%)
    ppermute x126, waiting for transfers between devices, shifted(): lax.ppermute(x, axis, [(i, (i + by) % devices) for i in range(devices)])  1410 us
    unnamed x9, waiting for transfers between devices  680 us
    dot_general x128, matrix products, pair_terms(): jnp.dot(weights, piece, preferred_element_type=jnp.float32)  101 us
  transfers between devices with their start and end apart: 131, of which 130 were waited for; matrix products, arithmetic and copies ran while one was open for 3% of the time, Pallas kernels for 0%

commit v1 on v0

v1 whole, which is shorter than its diff:
```python
import types

import jax
import jax.numpy as jnp
from jax import lax
from jax.experimental import pallas as pl
from jax.experimental.pallas import tpu as pltpu
from jax.sharding import PartitionSpec as P

LOGIT_SCALE = 10.0
LOGIT_BIAS = -2.5
NORM_EPS = 1e-06

NX = 4
NY = 4
NZ = 2
NC = 2
D = 1152
HALF = D // 2
PAIRS = 208
OWN = PAIRS // 2
WIN = 112
STEP = PAIRS - WIN
TC = NZ * WIN
IMGS = NX * PAIRS
YROWS = D // NY
ZROWS = YROWS // NZ
LAST = ZROWS // (NX * NC)
FIN = 32

NN = ((1,), (0,))
NT = ((1,), (1,))
TN = ((0,), (0,))
BF = jnp.bfloat16
F32 = jnp.float32

SCRATCH = {
    "nhf": ((PAIRS, HALF), F32),
    "nhb": ((PAIRS, HALF), BF),
    "rs": ((PAIRS, 128), F32),
    "tpart": ((PAIRS, D), F32),
    "tsend": ((WIN, D), BF),
    "trecv": ((WIN, D), BF),
    "u": ((2, 8, D), F32),
    "tproj": ((WIN, D), F32),
    "tsc": ((WIN, 128), F32),
    "ih": ((2, PAIRS, HALF), BF),
    "iproj": ((PAIRS, D), BF),
    "isc": ((PAIRS, 128), F32),
    "img": ((IMGS, D), BF),
    "txt": ((NY, NC, TC, D), BF),
    "w": ((NY, NC, IMGS, TC), BF),
    "gi": ((IMGS, D), F32),
    "xsend": ((NX, PAIRS, D), BF),
    "xrecv": ((NX, PAIRS, D), BF),
    "gtcsend": ((NY, TC, D), BF),
    "gtcrecv": ((NY, TC, D), BF),
    "gt": ((TC, D), F32),
    "gtsum": ((TC, D), F32),
    "ysend": ((NY, TC, D), BF),
    "yrecv": ((NY, TC, D), BF),
    "zsend": ((WIN, D), BF),
    "zrecv": ((WIN, D), BF),
    "tw": ((2, WIN, D), BF),
    "sw": ((2, WIN, 128), F32),
    "tpg": ((PAIRS, D), BF),
    "sec": ((PAIRS, 128), F32),
    "ghalf": ((PAIRS, HALF), F32),
    "izsend": ((PAIRS, HALF), BF),
    "izrecv": ((PAIRS, HALF), BF),
    "dots": ((2, PAIRS, 128), F32),
    "pg": ((PAIRS, HALF), BF),
    "gip": ((PAIRS, D), F32),
    "gsend": ((PAIRS, HALF), BF),
    "grecv": ((PAIRS, HALF), BF),
    "hs": ((NC, D, HALF), BF),
    "hcrecv": ((D, HALF), BF),
    "hysend": ((D, HALF), BF),
    "hyrecv": ((NY, YROWS, HALF), BF),
    "hown": ((YROWS, HALF), F32),
    "hzsend": ((ZROWS, HALF), BF),
    "hzrecv": ((ZROWS, HALF), BF),
    "hx": ((ZROWS, HALF), BF),
    "fin": ((NC, NX, FIN, HALF), BF),
}

SENDS = {}
total_sends = 0
for group, many in (
    ("t", 1), ("u", 1), ("ih", 1), ("img", NX), ("txty", NY), ("txtz", 1), ("txty2", NY), ("txtc", NY),
    ("x", NX), ("iz", 1), ("dots", 1), ("gtc", NY), ("y", NY), ("z", 1), ("tw", 1), ("sw", 1), ("g", 1),
    ("hc", 1), ("hy", NY), ("hz", 1), ("fin", NX * NC),
):
    SENDS[group] = total_sends
    total_sends += many

RECVS = {}
total_recvs = 0
for group, many in (
    ("t", 1), ("u", 1), ("ih", 1), ("img", NX), ("txt", NY * NZ), ("txtc", NY),
    ("x", NX), ("iz", 1), ("dots", 1), ("gtc", NY), ("y", NY), ("z", 1), ("tw", 1), ("sw", 1), ("g", 1),
    ("hc", 1), ("hy", NY), ("hz", 1), ("fin", NX * NC),
):
    RECVS[group] = total_recvs
    total_recvs += many


def dot(a, b, dims):
    return lax.dot_general(a, b, (dims, ((), ())), preferred_element_type=F32)


def rows(i, first=0):
    return pl.ds(pl.multiple_of(first + i * 16, 16), 16)


def rowsum(v):
    return jnp.sum(v, -1, keepdims=True)


def wide(v):
    return jnp.broadcast_to(v, (v.shape[0], 128))


def each(count, body):
    lax.fori_loop(0, count, lambda i, c: (body(i), c)[1], 0)


def kernel(img_feat, img_head, txt_feat, txt_head, g_img, g_ih, g_txt, g_th, *scratch):
    s = types.SimpleNamespace(**dict(zip(SCRATCH, scratch)))
    ssem, rsem = scratch[len(SCRATCH) :]
    dp, m = lax.axis_index("dp"), lax.axis_index("mp")
    core = lax.rem(dp, NC)
    x = lax.rem(dp // NC, NX)
    zh = lax.rem(dp // (NC * NX), NZ)
    y = dp // (NC * NX * NZ)
    om, oc, oz = 1 - m, 1 - core, 1 - zh

    def dev(yy=None, zz=None, xx=None, cc=None, mm=None):
        yy = y if yy is None else yy
        zz = zh if zz is None else zz
        xx = x if xx is None else xx
        cc = core if cc is None else cc
        mm = m if mm is None else mm
        return (((yy * NZ + zz) * NX + xx) * NC + cc, mm)

    mate, twin, far = dev(mm=om), dev(cc=oc), dev(zz=oz)

    def copy(src, dst, group, send_at, recv_at, to, recv_group=None):
        return pltpu.make_async_remote_copy(
            src_ref=src,
            dst_ref=dst,
            send_sem=ssem.at[SENDS[group] + send_at],
            recv_sem=rsem.at[RECVS[recv_group or group] + recv_at],
            device_id=to,
            device_id_type=pl.DeviceIdType.MESH,
        )

    def other(base, by, size):
        return lax.rem(base + by, size)

    def pick(whole, which):
        return jnp.where(which == 0, whole[:, :HALF], whole[:, HALF:])

    barrier = pltpu.get_barrier_semaphore()
    friends = [mate, twin, far]
    friends += [dev(yy=other(y, d, NY)) for d in range(1, NY)]
    friends += [dev(xx=other(x, d, NX), cc=c) for d in range(1, NX) for c in (core, oc)]
    for friend in friends:
        pl.semaphore_signal(barrier, inc=1, device_id=friend, device_id_type=pl.DeviceIdType.MESH)

    def norm(i):
        r = rows(i)
        t = txt_feat[r, :].astype(F32)
        c = t - rowsum(t) * (1.0 / D)
        rs = lax.rsqrt(rowsum(c * c) * (1.0 / D) + NORM_EPS)
        half = pick(c * rs, m)
        s.nhf[r, :] = half
        s.nhb[r, :] = half.astype(BF)
        s.rs[r, :] = wide(rs)

    each(PAIRS // 16, norm)
    s.tpart[...] = dot(s.nhb[...], txt_head[...], NN)

    def tosend(i):
        s.tsend[rows(i), :] = s.tpart[rows(i, om * STEP), :].astype(BF)

    each(WIN // 16, tosend)
    pl.semaphore_wait(barrier, len(friends))
    t_copy = copy(s.tsend, s.trecv, "t", 0, 0, mate)
    t_copy.start()
    s.u[m] = dot(jnp.ones((8, HALF), BF), txt_head[...], NN)
    u_copy = copy(s.u.at[m], s.u.at[m], "u", 0, 0, mate)
    u_copy.start()

    s.ih[m] = dot(img_feat[...], img_head[...], NN).astype(BF)
    ih_copy = copy(s.ih.at[m], s.ih.at[m], "ih", 0, 0, mate)
    ih_copy.start()

    t_copy.wait_recv()

    def embed_text(i):
        p = s.tpart[rows(i, m * STEP), :] + s.trecv[rows(i), :].astype(F32)
        sc = lax.rsqrt(rowsum(p * p) + NORM_EPS)
        row = m * STEP + i * 16 + lax.broadcasted_iota(jnp.int32, (16, 1), 0)
        mine = (row >= m * OWN) & (row < m * OWN + OWN)
        s.tproj[rows(i), :] = p
        s.tsc[rows(i), :] = wide(sc)
        s.txt[y, core, rows(i, zh * WIN), :] = jnp.where(mine, p * sc, 0.0).astype(BF)

    each(WIN // 16, embed_text)

    def part(yy, zz):
        return s.txt.at[yy, core, pl.ds(pl.multiple_of(zz * WIN, 16), WIN)]

    def text_y(d):
        yy = other(y, d, NY)
        return copy(part(y, zh), part(y, zh), "txty", d, y * NZ + zh, dev(yy=yy), "txt")

    def text_y2(d):
        yy = other(y, d, NY)
        return copy(part(y, oz), part(y, oz), "txty2", d, y * NZ + oz, dev(yy=yy), "txt")

    def text_c(k, yy):
        return copy(s.txt.at[yy, core], s.txt.at[yy, core], "txtc", k, yy, twin)

    def text_arrival(yy, zz):
        return copy(part(yy, zz), part(yy, zz), "txty", 0, yy * NZ + zz, far, "txt")

    text_z = copy(part(y, zh), part(y, zh), "txtz", 0, y * NZ + zh, far, "txt")
    text_z.start()
    for d in (1, 3, 2):
        text_y(d).start()

    ih_copy.wait_recv()

    def embed_image(i):
        r = rows(i)
        p = jnp.concatenate([s.ih[0, r, :].astype(F32), s.ih[1, r, :].astype(F32)], axis=1)
        sc = lax.rsqrt(rowsum(p * p) + NORM_EPS)
        s.iproj[r, :] = p.astype(BF)
        s.isc[r, :] = wide(sc)
        s.img[rows(i, x * PAIRS), :] = (p * sc).astype(BF)

    each(PAIRS // 16, embed_image)

    def images(xx):
        return pl.ds(pl.multiple_of(xx * PAIRS, 16), PAIRS)

    def image_copy(d, slot, to):
        return copy(s.img.at[images(slot)], s.img.at[images(slot)], "img", d, slot, to)

    for d in (1, 3, 2):
        image_copy(d, x, dev(xx=other(x, d, NX))).start()

    def zero(i):
        s.gi[rows(i), :] = jnp.zeros((16, D), F32)

    each(IMGS // 16, zero)
    text_arrival(y, oz).wait_recv()
    for d in (1, 3, 2):
        text_y2(d).start()
    text_c(0, y).start()

    def order(k):
        return k + k // 2 - 2 * (k // 3)

    def block(step):
        k, h = step // 2, lax.rem(step, 2)
        yy = other(y, order(k), NY)
        cc = lax.rem(core + h, NC)

        @pl.when((h == 0) & (k > 0))
        def _():
            text_arrival(yy, 0).wait_recv()
            text_arrival(yy, 1).wait_recv()
            text_c(k, yy).start()

        @pl.when(h == 1)
        def _():
            copy(s.txt.at[yy, oc], s.txt.at[yy, oc], "txtc", 0, yy, twin).wait_recv()

        delta = jnp.where(step == 0, x * PAIRS + m * STEP - zh * WIN, 1 << 20)

        def piece(j):
            xx = other(x, order(j), NX)

            @pl.when((step == 0) & (j > 0))
            def _():
                image_copy(0, xx, twin).wait_recv()

            texts = s.txt[yy, cc]
            scores = dot(s.img[images(xx), :], texts, NT)
            weights = 0.5 + 0.5 * jnp.tanh((0.5 * LOGIT_SCALE) * scores + 0.5 * LOGIT_BIAS)
            row = xx * PAIRS + lax.broadcasted_iota(jnp.int32, (PAIRS, TC), 0)
            col = lax.broadcasted_iota(jnp.int32, (PAIRS, TC), 1)
            match = (row - col == delta) & (col >= zh * WIN) & (col < zh * WIN + WIN)
            weights = (weights - match.astype(F32)).astype(BF)
            s.w[yy, cc, images(xx), :] = weights
            s.gi[images(xx), :] += dot(weights, texts, NN)

        each(NX, piece)

    each(NY * NC, block)

    def image_back(d, slot, to):
        return copy(s.xsend.at[slot], s.xrecv.at[x], "x", d, x, to)

    for d in (2, 1, 3):
        xx = other(x, d, NX)

        def cast(i, xx=xx):
            s.xsend[xx, rows(i), :] = s.gi[rows(i, xx * PAIRS), :].astype(BF)

        each(PAIRS // 16, cast)
        image_back(d, xx, dev(xx=xx)).start()

    def text_back_c(yy):
        return copy(s.gtcsend.at[yy], s.gtcrecv.at[yy], "gtc", yy, yy, twin)

    def text_back_y(d, yy, to):
        return copy(s.ysend.at[yy], s.yrecv.at[y], "y", d, y, to)

    def text_grad(k):
        d = lax.rem(2 + 2 * NY - order(k), NY)
        d = jnp.where(k == 3, 0, jnp.where(k == 0, 2, 2 * k - 1))
        yy = other(y, d, NY)
        s.gtcsend[yy] = dot(s.w[yy, oc], s.img[...], TN).astype(BF)
        text_back_c(yy).start()
        s.gt[...] = dot(s.w[yy, core], s.img[...], TN)
        text_back_c(yy).wait_recv()

        @pl.when(k < 3)
        def _():
            def add(i):
                s.ysend[yy, rows(i), :] = (s.gt[rows(i), :] + s.gtcrecv[yy, rows(i), :].astype(F32)).astype(BF)

            each(TC // 16, add)
            text_back_y(d, yy, dev(yy=yy)).start()

        @pl.when(k == 3)
        def _():
            def add(i):
                s.gtsum[rows(i), :] = s.gt[rows(i), :] + s.gtcrecv[yy, rows(i), :].astype(F32)

            each(TC // 16, add)

    each(NY, text_grad)

    for d in (1, 3, 2):
        copy(s.xsend.at[0], s.xrecv.at[other(x, d, NX)], "x", 0, other(x, d, NX), twin).wait_recv()

    def image_sum(i):
        r = rows(i)
        g = s.gi[rows(i, x * PAIRS), :]
        for d in (1, 3, 2):
            g = g + s.xrecv[other(x, d, NX), r, :].astype(F32)
        g = LOGIT_SCALE * g
        s.dots[m, r, :] = wide(rowsum(g * s.iproj[r, :].astype(F32)))
        s.ghalf[r, :] = pick(g, m)
        s.izsend[r, :] = pick(g, om).astype(BF)

    each(PAIRS // 16, image_sum)
    iz_copy = copy(s.izsend, s.izrecv, "iz", 0, 0, mate)
    dots_copy = copy(s.dots.at[m], s.dots.at[m], "dots", 0, 0, mate)
    dots_copy.start()
    iz_copy.start()

    for d in (1, 3, 2):
        copy(s.ysend.at[0], s.yrecv.at[other(y, d, NY)], "y", 0, other(y, d, NY), twin).wait_recv()

    def text_sum(r):
        g = s.gtsum[r, :]
        for d in (1, 3, 2):
            g = g + s.yrecv[other(y, d, NY), r, :].astype(F32)
        return g

    def text_far(i):
        s.zsend[rows(i), :] = text_sum(rows(i, oz * WIN)).astype(BF)

    each(WIN // 16, text_far)
    z_copy = copy(s.zsend, s.zrecv, "z", 0, 0, far)
    z_copy.start()

    def text_near(i):
        s.gt[rows(i), :] = text_sum(rows(i, zh * WIN))

    each(WIN // 16, text_near)

    dots_copy.wait_recv()
    iz_copy.wait_recv()

    def image_grad(i):
        r = rows(i)
        g = s.ghalf[r, :] + s.izrecv[r, :].astype(F32)
        sc = s.isc[r, :][:, :1]
        total = (s.dots[0, r, :] + s.dots[1, r, :])[:, :1]
        p = pick(s.iproj[r, :].astype(F32), m)
        s.pg[r, :] = (sc * g - (sc * sc * sc) * p * total).astype(BF)

    each(PAIRS // 16, image_grad)
    s.gip[...] = dot(s.pg[...], img_head[...], NT)

    def image_out(i):
        s.gsend[rows(i), :] = pick(s.gip[rows(i), :], om).astype(BF)

    each(PAIRS // 16, image_out)
    g_copy = copy(s.gsend, s.grecv, "g", 0, 0, mate)

    z_copy.wait_recv()

    def text_own(i):
        r = rows(i)
        g = LOGIT_SCALE * (s.gt[r, :] + s.zrecv[r, :].astype(F32))
        p = s.tproj[r, :]
        sc = s.tsc[r, :][:, :1]
        v = sc * g - (sc * sc * sc) * p * rowsum(p * g)
        row = m * STEP + i * 16 + lax.broadcasted_iota(jnp.int32, (16, 1), 0)
        mine = (row >= m * OWN) & (row < m * OWN + OWN)
        v = jnp.where(mine, v, 0.0).astype(BF)
        s.tw[m, r, :] = v
        s.sw[m, r, :] = wide(rowsum(v.astype(F32) * p))

    each(WIN // 16, text_own)
    tw_copy = copy(s.tw.at[m], s.tw.at[m], "tw", 0, 0, mate)
    sw_copy = copy(s.sw.at[m], s.sw.at[m], "sw", 0, 0, mate)
    tw_copy.start()
    sw_copy.start()
    g_copy.start()
    s.hs[0] = dot(img_feat[...], s.pg[...], TN).astype(BF)
    tw_copy.wait_recv()
    sw_copy.wait_recv()
    u_copy.wait_recv()

    def merge(i):
        lo, hi = jnp.minimum(i, 6), jnp.maximum(i - 6, 0)
        v = jnp.where(i <= 6, s.tw[0, rows(lo), :].astype(F32), 0.0)
        v = v + jnp.where(i >= 6, s.tw[1, rows(hi), :].astype(F32), 0.0)
        s.tpg[rows(i), :] = v.astype(BF)
        v = jnp.where(i <= 6, s.sw[0, rows(lo), :], 0.0)
        s.sec[rows(i), :] = v + jnp.where(i >= 6, s.sw[1, rows(hi), :], 0.0)

    each(PAIRS // 16, merge)
    s.hs[1] = dot(s.tpg[...], s.nhb[...], TN).astype(BF)
    hc_copy = copy(s.hs.at[oc], s.hcrecv, "hc", 0, 0, twin)
    hc_copy.start()

    g_txt[...] = dot(s.tpg[...], txt_head[...], NT)

    def text_input(i):
        r = rows(i)
        u = (s.u[0] + s.u[1])[:1, :]
        first = rowsum(s.tpg[r, :].astype(F32) * u) * (1.0 / D)
        second = s.sec[r, :][:, :1] * (1.0 / D)
        g_txt[r, :] = s.rs[r, :][:, :1] * (g_txt[r, :] - first - s.nhf[r, :] * second)

    each(PAIRS // 16, text_input)

    hc_copy.wait_recv()

    def head_sum(r):
        return s.hs[core, r, :].astype(F32) + s.hcrecv[r, :].astype(F32)

    def head_y(d, to):
        yy = other(y, d, NY)
        src = s.hysend.at[pl.ds(pl.multiple_of(yy * YROWS, 16), YROWS)]
        return copy(src, s.hyrecv.at[y], "hy", d, y, to)

    for d in (2, 1, 3):
        yy = other(y, d, NY)

        def cast_head(i, yy=yy):
            r = rows(i, yy * YROWS)
            s.hysend[r, :] = head_sum(r).astype(BF)

        each(YROWS // 16, cast_head)
        head_y(d, dev(yy=yy)).start()

    def head_own(i):
        s.hown[rows(i), :] = head_sum(rows(i, y * YROWS))

    each(YROWS // 16, head_own)

    g_copy.wait_recv()

    def image_input(i):
        r = rows(i)
        g_img[r, :] = pick(s.gip[r, :], m) + s.grecv[r, :].astype(F32)

    each(PAIRS // 16, image_input)

    for d in (1, 3, 2):
        yy = other(y, d, NY)
        copy(s.hyrecv.at[0], s.hyrecv.at[yy], "hy", 0, yy, twin).wait_recv()

    def head_all(r):
        g = s.hown[r, :]
        for d in (1, 3, 2):
            g = g + s.hyrecv[other(y, d, NY), r, :].astype(F32)
        return g

    def head_far(i):
        s.hzsend[rows(i), :] = head_all(rows(i, oz * ZROWS)).astype(BF)

    each(ZROWS // 16, head_far)
    hz_copy = copy(s.hzsend, s.hzrecv, "hz", 0, 0, far)
    hz_copy.start()

    def head_near(i):
        r = rows(i, zh * ZROWS)
        s.hown[r, :] = head_all(r)

    each(ZROWS // 16, head_near)
    hz_copy.wait_recv()

    def head_last(i):
        v = s.hown[rows(i, zh * ZROWS), :] + s.hzrecv[rows(i), :].astype(F32)
        s.hx[rows(i), :] = v.astype(BF)

    each(ZROWS // 16, head_last)

    def window(xx, cc):
        return pl.ds(pl.multiple_of((xx * NC + cc) * 16, 16), FIN)

    def fin_copy(xx, cc):
        at = xx * NC + cc
        return copy(s.hx.at[window(xx, cc)], s.fin.at[core, x], "fin", at, core * NX + x, dev(xx=xx, cc=cc))

    others = [(other(x, d, NX), c) for d in range(NX) for c in (core, oc)][1:]
    for xx, cc in others:
        fin_copy(xx, cc).start()
    s.fin[core, x] = s.hx[window(x, core), :]
    for xx, cc in others:
        copy(s.fin.at[cc, xx], s.fin.at[cc, xx], "fin", 0, cc * NX + xx, twin).wait_recv()

    skip = lax.rem(FIN - 2 * (x * NC + core), FIN)

    def last(head):
        v = s.fin[head, 0].astype(F32)
        for xx in range(1, NX):
            v = v + s.fin[head, xx].astype(F32)
        return pltpu.roll(v, skip, 0)

    g_ih[...] = last(0)[:LAST, :]
    g_th[...] = jnp.transpose(last(1))[:, :LAST]

    for c in (t_copy, u_copy, ih_copy, text_z, iz_copy, dots_copy, z_copy, tw_copy, sw_copy, g_copy, hc_copy, hz_copy):
        c.wait_send()
    for d in range(1, 4):
        text_y(d).wait_send()
        text_y2(d).wait_send()
        image_copy(d, x, twin).wait_send()
        image_back(d, other(x, d, NX), twin).wait_send()
        text_back_y(d, other(y, d, NY), twin).wait_send()
        head_y(d, twin).wait_send()
    for k in range(NY):
        text_c(k, y).wait_send()
        text_back_c(other(y, k, NY)).wait_send()
    for xx, cc in others:
        fin_copy(xx, cc).wait_send()


def per_device(img_feat, img_head, txt_feat, txt_head):
    vmem = pl.BlockSpec(memory_space=pltpu.VMEM)
    return pl.pallas_call(
        kernel,
        out_shape=(
            jax.ShapeDtypeStruct((PAIRS, HALF), F32),
            jax.ShapeDtypeStruct((LAST, HALF), F32),
            jax.ShapeDtypeStruct((PAIRS, HALF), F32),
            jax.ShapeDtypeStruct((HALF, LAST), F32),
        ),
        in_specs=[vmem] * 4,
        out_specs=(vmem,) * 4,
        scratch_shapes=[pltpu.VMEM(shape, kind) for shape, kind in SCRATCH.values()]
        + [pltpu.SemaphoreType.DMA((total_sends,)), pltpu.SemaphoreType.DMA((total_recvs,))],
        compiler_params=pltpu.CompilerParams(
            collective_id=0, has_side_effects=True, vmem_limit_bytes=60 * 1024 * 1024
        ),
        cost_estimate=pl.CostEstimate(flops=14 * 10**9, bytes_accessed=5 * 10**6, transcendentals=0),
    )(img_feat, img_head, txt_feat, txt_head)


def solution(mesh):
    in_specs = (P("dp", None), P(None, "mp"), P("dp", None), P("mp", None))
    out_specs = (P("dp", "mp"), P("dp", "mp"), P("dp", "mp"), P("mp", "dp"))
    return jax.shard_map(
        per_device, mesh=mesh, in_specs=in_specs, out_specs=out_specs, check_vma=False
    )
```

time: 2340 us -> 169 us (0.07)
  waiting for transfers between devices: 2090 us -> 0 us
  Pallas kernels: 0 us -> 160 us
  matrix products: 111 us -> 0 us
  local copies, waits for them, and re-layouts: 54.4 us -> 7.71 us
  blocking collectives: 28.4 us -> 0 us
    ppermute x126 -> x0, waiting for transfers between devices: 1410 us -> none  [shifted(): lax.ppermute(x, axis, [(i, (i + by) % devices) for i in range(devices)])]
    unnamed x9 -> x0, waiting for transfers between devices: 680 us -> none
    pallas_call x0 -> x1, Pallas kernels: none -> 160 us  [per_device(): pl.pallas_call(kernel, out_shape=(jax.ShapeDtypeStruct((PAIRS, HALF), F32...]
    dot_general x134 -> x0, matrix products: 111 us -> none  [the longest x128 101 us: pair_terms(): jnp.dot(weights, piece, preferred_element_type=jnp.float32)]
    while x126 -> x0, local copies, waits for them, and re-layouts: 44.7 us -> none
    all_gather x3 -> x0, blocking collectives: 24.2 us -> none  [the longest x1 9.21 us: per_device(): img_proj = lax.all_gather(img_half, 'mp', axis=1, tiled=True)]
  transfers between devices with their start and end apart: 131 -> 0, of which waited for: 130 -> 0; matrix products, arithmetic and copies ran while one was open for 3% -> 0% of each run, Pallas kernels for 0% -> 0%
where the time goes in v1:
time: 169 us
  Pallas kernels  160 us (95%)
  local copies, waits for them, and re-layouts  7.71 us (5%)
    pallas_call x1, Pallas kernels, per_device(): pl.pallas_call(kernel, out_shape=(jax.ShapeDtypeStruct((PAIRS, HALF), F32...  160 us
    unnamed x8, local copies, waits for them, and re-layouts  5.92 us

profile of v1, /device:TPU:1, one launch (start us, length us, event | category | flops | bytes accessed | tf_op | source)
XLA Modules:
  0.0 168.8 jit_solution(17065102434365743611)
XLA Ops:
  0.6 2.6 %copy.8.img_head = bf16[1152,576]{1,0:T(8,128)(2,1)} copy(bf16[1152,576]{0,1:T(8,128)(2,1)} %param.5) | data formatting | bytes 2654208 | tf_op args[1]
  3.2 160.4 %shard_map.75 = (f32[208,576]{1,0:T(8,128)}, f32[18,576]{1,0:T(8,128)}, f32[208,576]{1,0:T(8,128)}, f32[576,18]{1,0:T(8,128)}) custom-call(bf16[208,1152]{1,0:T(8,128)(2,1)} %img_feat.1, bf16[1152,576]{1,0:T(8,128)(2,1)} %copy.8.img_head, bf16[208,1152]{1,0:T(8,128)(2,1)} %txt_feat.1, bf16[576,1152]{1,0:T(8,128)(2,1)} %txt_head.1), custom_call_target="tpu_custom_call" | custom-call | flops 14000000000 | bytes 5000000 | tf_op jit(solution)/shard_map/pallas_call | solution.py:564
  163.7 0.0 copy-start.1
  163.7 0.0 copy-start
  163.7 1.8 %copy.9 = f32[576,18]{0,1:T(8,128)} copy(f32[576,18]{1,0:T(8,128)} %get-tuple-element.7) | data formatting | bytes 82944 | tf_op jit(solution)/shard_map/pallas_call | solution.py:564
  165.5 1.9 %copy.13 = f32[208,576]{1,0:T(8,128)} copy(f32[208,576]{1,0:T(8,128)} %get-tuple-element.12) | data formatting | bytes 958464
  167.3 0.0 copy-done.1
  167.4 0.6 copy.14
  168.0 0.0 copy-done
  168.0 0.8 copy.15
Async XLA Ops:
  163.7 3.7 %copy-start.1 = (f32[18,576]{1,0:T(8,128)S(1)}, f32[18,576]{1,0:T(8,128)}, u32[]{:S(2)}) copy-start(f32[18,576]{1,0:T(8,128)} %get-tuple-element.13) | copy-start | bytes 124420
  163.7 4.3 %copy-start = (f32[208,576]{1,0:T(8,128)S(1)}, f32[208,576]{1,0:T(8,128)}, u32[]{:S(2)}) copy-start(f32[208,576]{1,0:T(8,128)} %get-tuple-element.14) | copy-start | bytes 1437700
